TPU v7x, 32 devices: a whole 2x2x4 slice. The times are simulated.
32 devices in a mesh: gx: 4 (over y, core), gy: 8 (over z, x).
Axes of the slice: x: 2, y: 2, z: 4, core: 2. Of those that a mesh axis runs over, the one named last changes fastest.
Arguments:
- entity_table: float32 [8192, 256], P(('gx', 'gy')), may hold values from -2.5 to 2.5
- relations: float32 [4, 256, 256], replicated, may hold values from -0.375 to 0.375
- rel_ids: int32 [3, 128], P(None, ('gx', 'gy')), may hold values from 0 to 3
- edge_src: int32 [3, 196608], P(None, ('gx', 'gy')), may hold values from 0 to 255
- edge_dst: int32 [3, 196608], P(None, ('gx', 'gy')), may hold values from 0 to 255
Outputs:
- new_table: float32 [8192, 256], P(('gx', 'gy'))
- rel_grad: float32 [4, 256, 256], replicated
All inputs are finite; a program needn't handle non-finite values.
Results may differ from a plain program's by a relative error of at most 0.0089.
Values may be sent and summed in bfloat16 or wider, within the bound.
A program may use at most 64 MiB of HBM per device.

v0:
```python
import math

import jax
import jax.numpy as jnp
from jax import lax
from jax.sharding import PartitionSpec as P

learn_rate = 0.5
highest = lax.Precision.HIGHEST


def passed_along(value, axis, steps):
    count = lax.axis_size(axis)
    pairs = [(source, (source + steps) % count) for source in range(count)]
    return lax.ppermute(value, axis, pairs)


def fetch_rows(values, axis_name, offset):
    if axis_name == "gy":
        return passed_along(values, "gy", offset)
    return passed_along(values, "gx", offset)


def return_rows(values, axis_name, offset):
    if axis_name == "gy":
        return passed_along(values, "gy", offset)
    return passed_along(values, "gx", offset)


def slope_matrix(mapped_flat, dst_b, sources, targets):
    scores = lax.dot_general(
        mapped_flat, dst_b, (((1,), (1,)), ((), ())), preferred_element_type=jnp.float32
    )
    scaling = 1.0 / math.sqrt(mapped_flat.shape[0])
    slopes = jax.nn.sigmoid(scores) * scaling
    slopes = slopes.at[sources, targets].add(-scaling)
    return slopes.astype(jnp.bfloat16)


def column_product(slopes_b, mapped_flat):
    return lax.dot_general(
        slopes_b, mapped_flat, (((0,), (0,)), ((), ())), preferred_element_type=jnp.float32
    ).astype(jnp.bfloat16)


def shards(entity_table, relations, rel_ids, edge_src, edge_dst):
    entity = entity_table
    row_count, feature = entity.shape
    rounds_total = rel_ids.shape[0]
    group_count = rel_ids.shape[1]
    kinds = relations.shape[0]
    block_rows = row_count // group_count
    buckets = (("gy", 1), ("gx", 1), ("gy", -1))
    rel_total = jnp.zeros(relations.shape, jnp.float32)
    for turn_index in range(rounds_total):
        axis_name, offset = buckets[turn_index % 3]
        own_b = entity.astype(jnp.bfloat16)
        dst_b = fetch_rows(own_b, axis_name, offset)
        selector = (
            rel_ids[turn_index][:, None] == jnp.arange(kinds, dtype=jnp.int32)[None, :]
        ).astype(jnp.float32)
        chosen = jnp.einsum("gk,kde->gde", selector, relations, precision=highest).astype(
            jnp.bfloat16
        )
        src_b = own_b.reshape(group_count, block_rows, feature)
        mapped = jnp.einsum(
            "gsd,gde->gse", src_b, chosen, preferred_element_type=jnp.float32
        ).astype(jnp.bfloat16)
        mapped_flat = mapped.reshape(row_count, feature)
        sources = edge_src[turn_index]
        targets = edge_dst[turn_index]
        slopes_b = slope_matrix(mapped_flat, dst_b, sources, targets)
        pulled = jnp.dot(slopes_b, dst_b, preferred_element_type=jnp.float32).astype(jnp.bfloat16)
        pulled = pulled.reshape(group_count, block_rows, feature)
        src_grad = jnp.einsum(
            "gse,gde->gsd", pulled, chosen, preferred_element_type=jnp.float32
        ).reshape(row_count, feature)
        rel_group = jnp.einsum("gsd,gse->gde", src_b, pulled, preferred_element_type=jnp.float32)
        rel_part = jnp.einsum("gk,gde->kde", selector, rel_group, precision=highest)
        dst_grad = column_product(slopes_b, mapped_flat)
        returned = return_rows(dst_grad, axis_name, -offset)
        entity = entity - learn_rate * (src_grad + returned.astype(jnp.float32))
        rel_total = rel_total + rel_part
    rel_total = lax.psum(rel_total, ("gx", "gy"))
    divisor = math.sqrt(rounds_total * lax.axis_size("gx") * lax.axis_size("gy"))
    return (entity, rel_total / divisor)


def solution(mesh):
    return jax.shard_map(
        shards,
        mesh=mesh,
        in_specs=(
            P(("gx", "gy"), None),
            P(),
            P(None, ("gx", "gy")),
            P(None, ("gx", "gy")),
            P(None, ("gx", "gy")),
        ),
        out_specs=(P(("gx", "gy"), None), P()),
        check_vma=False,
    )
```

profile of v0, /device:TPU:0, one launch (start us, length us, event | category | flops | bytes accessed | tf_op | source)
XLA Modules:
  0.0 294.8 jit_solution(986768562513324960)
XLA Ops:
  7.2 0.0 all-reduce.2.cloned.1.call-start
  7.3 1.1 convert_element_type.70
  8.3 3.0 %collective-permute-start = (bf16[256,256]{1,0:T(8,128)(2,1)S(1)}, bf16[256,256]{1,0:T(8,128)(2,1)S(1)}, u32[]{:S(2)}, u32[]{:S(2)}) collective-permute-start(bf16[256,256]{1,0:T(8,128)(2,1)S(1)} %convert_element_type.70), channel_id=1, source_target_pairs={{0,1},{1,2},{2,3},{3,4},{4,5},{5,6},{6,7},{7,0},{8,9},{9,10},{10,1... | collective-permute-start | bytes 393224 | tf_op jit(solution)/shard_map/ppermute | solution.py:15
  11.3 0.2 compare_select_fusion.2
  11.5 0.1 and_reduce_fusion.2
  11.6 0.1 and_reduce_fusion.1
  11.8 0.1 and_reduce_fusion
  11.9 0.5 copy-done.13
  12.4 0.3 multiply_reduce_fusion
  12.7 1.9 convolution_convert_fusion.2
  14.6 1.9 convolution_convert_fusion.1
  16.5 1.9 convolution_convert_fusion
  18.4 0.2 convolution_convert_fusion.3
  18.6 0.6 broadcast_select_fusion.1
  19.2 0.6 broadcast_select_fusion
  19.8 0.3 fusion.14
  20.1 0.1 copy.42
  20.3 0.6 copy-done.5
  20.9 33.4 %scatter_fusion = f32[65536]{0:T(1024)S(1)} fusion(f32[65536]{0:T(1024)S(1)} %bitcast.110, s32[6144]{0:T(1024)S(1)} %broadcast_select_fusion.2, f32[6144]{0:T(1024)S(1)} %broadcast.134), kind=kCustom, calls=%fused_computation | custom fusion | flops 6144 | bytes 98304
  54.4 0.9 convolution_convert_fusion.10
  55.2 3.1 %collective-permute-start.1 = (bf16[256,256]{1,0:T(8,128)(2,1)}, bf16[256,256]{1,0:T(8,128)(2,1)S(1)}, u32[]{:S(2)}, u32[]{:S(2)}) collective-permute-start(bf16[256,256]{1,0:T(8,128)(2,1)} %convolution_convert_fusion.10), channel_id=1, source_target_pairs={{0,7},{1,0},{2,1},{3,2},{4,3},{5,4},{6,5},{7,6},{8,15},{9,8},{10,9... | collective-permute-start | bytes 393224 | tf_op jit(solution)/shard_map/ppermute | solution.py:15
  58.3 0.2 convolution_convert_fusion.11
  58.5 1.3 fusion.55
  59.8 2.5 copy.36
  62.4 3.2 %fusion.15 = f32[4,256,256]{2,0,1:T(4,128)} fusion(f32[4,256,256]{1,0,2:T(4,128)} %copy.36, s32[4]{0:T(128)S(1)} %get-tuple-element.18), kind=kOutput, calls=%fused_computation.35 | convolution fusion | flops 12582928 | bytes 2097168 | tf_op jit(solution)/shard_map/gk,gde->kde/dot_general | solution.py:79
  65.6 0.3 fusion.28
  65.9 0.7 copy-done.2
  66.6 0.1 collective-permute-start.2
  66.7 0.2 convolution_convert_fusion.5
  66.9 4.2 %collective-permute-done.2 = bf16[256,256]{1,0:T(8,128)(2,1)S(1)} collective-permute-done((bf16[256,256]{1,0:T(8,128)(2,1)S(1)}, bf16[256,256]{1,0:T(8,128)(2,1)S(1)}, u32[]{:S(2)}, u32[]{:S(2)}) %collective-permute-start.2) | collective-permute-done | bytes 131104 | tf_op jit(solution)/shard_map/ppermute | solution.py:15
  71.1 0.3 fusion.9
  71.4 0.1 copy.43
  71.5 0.6 copy-done.6
  72.1 0.0 copy-done.9
  72.1 33.6 %scatter_fusion.1 = f32[65536]{0:T(1024)S(1)} fusion(f32[65536]{0:T(1024)S(1)} %bitcast.112, s32[6144]{0:T(1024)S(1)} %copy-done.9, f32[6144]{0:T(1024)S(1)} %copy-done.6), kind=kCustom, calls=%fused_computation.1 | custom fusion | flops 6144 | bytes 98304
  105.8 0.2 convolution_convert_fusion.8
  106.0 0.1 collective-permute-start.3
  106.1 0.2 convolution_convert_fusion.9
  106.3 0.3 fusion.56
  106.6 0.4 copy-done.1
  107.0 1.8 convolution_add_fusion.1
  108.8 0.3 fusion.25
  109.1 0.7 copy-done.3
  109.8 0.8 fusion.53
  110.6 2.0 collective-permute-start.4
  112.6 0.2 convolution_convert_fusion.4
  112.8 3.9 %collective-permute-done.4 = bf16[256,256]{1,0:T(8,128)(2,1)S(1)} collective-permute-done((bf16[256,256]{1,0:T(8,128)(2,1)S(1)}, bf16[256,256]{1,0:T(8,128)(2,1)S(1)}, u32[]{:S(2)}, u32[]{:S(2)}) %collective-permute-start.4) | collective-permute-done | bytes 131104 | tf_op jit(solution)/shard_map/ppermute | solution.py:15
  116.7 0.3 fusion.4
  117.0 0.1 copy.44
  117.2 0.6 copy-done.7
  117.7 0.0 copy-done.8
  117.7 33.4 %scatter_fusion.2 = f32[65536]{0:T(1024)S(1)} fusion(f32[65536]{0:T(1024)S(1)} %bitcast.111, s32[6144]{0:T(1024)S(1)} %copy-done.8, f32[6144]{0:T(1024)S(1)} %copy-done.7), kind=kCustom, calls=%fused_computation.2 | custom fusion | flops 6144 | bytes 98304
  151.3 0.2 convolution_convert_fusion.7
  151.4 0.3 fusion.57
  151.8 2.7 convolution_add_fusion
  154.5 0.0 all-reduce.2.cloned.1.call-update
  154.5 0.2 convolution_convert_fusion.6
  154.7 0.1 collective-permute-start.5
  154.8 0.3 fusion.22
  155.1 7.7 %collective-permute-done.5 = bf16[256,256]{1,0:T(8,128)(2,1)S(1)} collective-permute-done((bf16[256,256]{1,0:T(8,128)(2,1)S(1)}, bf16[256,256]{1,0:T(8,128)(2,1)S(1)}, u32[]{:S(2)}, u32[]{:S(2)}) %collective-permute-start.5) | collective-permute-done | bytes 131104 | tf_op jit(solution)/shard_map/ppermute | solution.py:15
  162.8 0.7 fusion.32
  163.6 121.8 %all-reduce.2.cloned.1.call-done = f32[4,256,256]{2,0,1:T(4,128)} async-done(((f32[4,256,256]{2,0,1:T(4,128)}), f32[4,256,256]{2,0,1:T(4,128)}) %all-reduce.2.cloned.1.call-update) | async-done | bytes 1048592 | tf_op jit(solution)/shard_map/psum | solution.py:84
  285.3 1.5 broadcast_multiply_fusion
  286.8 1.2 copy.32
  (32 shorter events, 0.3 us)
Async XLA Ops:
  7.2 5.5 %copy-start = (f32[4,256,256]{2,1,0:T(8,128)S(1)}, f32[4,256,256]{2,1,0:T(8,128)}, u32[]{:S(2)}) copy-start(f32[4,256,256]{2,1,0:T(8,128)} %param.6) | copy-start | bytes 3145732
  7.2 4.1 %copy-start.12 = (s32[3,4]{1,0:T(4,128)S(1)}, s32[3,4]{1,0:T(4,128)}, u32[]{:S(2)}) copy-start(s32[3,4]{1,0:T(4,128)} %param.7) | copy-start | bytes 148
  7.2 4.1 %copy-start.10 = (s32[3,6144]{1,0:T(4,128)S(1)}, s32[3,6144]{1,0:T(4,128)}, u32[]{:S(2)}) copy-start(s32[3,6144]{1,0:T(4,128)} %param.9) | copy-start | bytes 221188
  7.2 4.1 %copy-start.11 = (s32[3,6144]{1,0:T(4,128)S(1)}, s32[3,6144]{1,0:T(4,128)}, u32[]{:S(2)}) copy-start(s32[3,6144]{1,0:T(4,128)} %param.8) | copy-start | bytes 221188
  7.2 278.1 %all-reduce.2.cloned.1.call-start = ((), (), s32[]{:S(2)}) async-start(), calls=%async_computation | async-start | bytes 2097152 | tf_op jit(solution)/shard_map/psum | solution.py:84
  8.3 11.5 %collective-permute-start = (bf16[256,256]{1,0:T(8,128)(2,1)S(1)}, bf16[256,256]{1,0:T(8,128)(2,1)S(1)}, u32[]{:S(2)}, u32[]{:S(2)}) collective-permute-start(bf16[256,256]{1,0:T(8,128)(2,1)S(1)} %convert_element_type.70), channel_id=1, source_target_pairs={{0,1},{1,2},{2,3},{3,4},{4,5},{5,6},{6,7},{7,0},{8,9},{9,10},{10,1... | collective-permute-start | bytes 393224 | tf_op jit(solution)/shard_map/ppermute | solution.py:15
  11.7 0.7 copy-start.13
  20.2 0.6 copy-start.5
  55.2 10.7 %collective-permute-start.1 = (bf16[256,256]{1,0:T(8,128)(2,1)}, bf16[256,256]{1,0:T(8,128)(2,1)S(1)}, u32[]{:S(2)}, u32[]{:S(2)}) collective-permute-start(bf16[256,256]{1,0:T(8,128)(2,1)} %convolution_convert_fusion.10), channel_id=1, source_target_pairs={{0,7},{1,0},{2,1},{3,2},{4,3},{5,4},{6,5},{7,6},{8,15},{9,8},{10,9... | collective-permute-start | bytes 393224 | tf_op jit(solution)/shard_map/ppermute | solution.py:15
  65.6 0.9 copy-start.2
  66.6 4.4 %collective-permute-start.2 = (bf16[256,256]{1,0:T(8,128)(2,1)S(1)}, bf16[256,256]{1,0:T(8,128)(2,1)S(1)}, u32[]{:S(2)}, u32[]{:S(2)}) collective-permute-start(bf16[256,256]{1,0:T(8,128)(2,1)S(1)} %fusion.37), channel_id=1, source_target_pairs={{0,8},{8,16},{16,24},{24,0},{1,9},{9,17},{17,25},{25,1},{2,10},{10... | collective-permute-start | bytes 393224 | tf_op jit(solution)/shard_map/ppermute | solution.py:15
  71.3 0.7 copy-start.6
  71.3 0.7 copy-start.9
  105.8 1.2 copy-start.1
  106.0 3.1 %collective-permute-start.3 = (bf16[256,256]{1,0:T(8,128)(2,1)S(1)}, bf16[256,256]{1,0:T(8,128)(2,1)S(1)}, u32[]{:S(2)}, u32[]{:S(2)}) collective-permute-start(bf16[256,256]{1,0:T(8,128)(2,1)S(1)} %convolution_convert_fusion.8), channel_id=1, source_target_pairs={{0,24},{8,0},{16,8},{24,16},{1,25},{9,1},{17,9},{25,17},{2,26},{10... | collective-permute-start | bytes 393224 | tf_op jit(solution)/shard_map/ppermute | solution.py:15
  108.8 1.0 copy-start.3
  110.6 6.2 %collective-permute-start.4 = (bf16[256,256]{1,0:T(8,128)(2,1)S(1)}, bf16[256,256]{1,0:T(8,128)(2,1)S(1)}, u32[]{:S(2)}, u32[]{:S(2)}) collective-permute-start(bf16[256,256]{1,0:T(8,128)(2,1)S(1)} %get-tuple-element.9), channel_id=1, source_target_pairs={{0,7},{1,0},{2,1},{3,2},{4,3},{5,4},{6,5},{7,6},{8,15},{9,8},{10,9... | collective-permute-start | bytes 393224 | tf_op jit(solution)/shard_map/ppermute | solution.py:15
  117.0 0.7 copy-start.7
  117.0 0.7 copy-start.8
  154.7 8.1 %copy-start.4 = (f32[256,256]{1,0:T(8,128)S(1)}, f32[256,256]{1,0:T(8,128)}, u32[]{:S(2)}) copy-start(f32[256,256]{1,0:T(8,128)} %get-tuple-element.10) | copy-start | bytes 786436
  154.7 8.1 %collective-permute-start.5 = (bf16[256,256]{1,0:T(8,128)(2,1)S(1)}, bf16[256,256]{1,0:T(8,128)(2,1)S(1)}, u32[]{:S(2)}, u32[]{:S(2)}) collective-permute-start(bf16[256,256]{1,0:T(8,128)(2,1)S(1)} %convolution_convert_fusion.6), channel_id=1, source_target_pairs={{0,1},{1,2},{2,3},{3,4},{4,5},{5,6},{6,7},{7,0},{8,9},{9,10},{10,1... | collective-permute-start | bytes 393224 | tf_op jit(solution)/shard_map/ppermute | solution.py:15
Sparse Core Ops, SparseCore 0:
  154.6 130.6 all-reduce.1
where the time goes:
time: 295 us
  waiting for transfers between devices  138 us (47%)
  other arithmetic  107 us (36%)
  matrix products  19.5 us (7%)
  between operations  14.5 us (5%)
  local copies, waits for them, and re-layouts  8.32 us (3%)
  starting transfers between devices  8.27 us (3%)
    psum x1, waiting for transfers between devices, shards(): rel_total = lax.psum(rel_total, ('gx', 'gy'))  122 us
    unnamed x10, other arithmetic  102 us
    ppermute x6, waiting for transfers between devices, passed_along(): return lax.ppermute(value, axis, pairs)  15.8 us
    ppermute x6, starting transfers between devices, passed_along(): return lax.ppermute(value, axis, pairs)  8.23 us
    dot_general x3, matrix products, shards(): rel_part = jnp.einsum('gk,gde->kde', selector, rel_group, precision=highest)  7.75 us
  transfers between devices with their start and end apart: 7, of which 4 were waited for; matrix products, arithmetic and copies ran while one was open for 7% of the time, Pallas kernels for 0%

commit v1 on v0

v1 whole, which is shorter than its diff:
```python
import functools
import math

import jax
import jax.numpy as jnp
from jax import lax
from jax.experimental import pallas as pl
from jax.experimental.pallas import tpu as pltpu
from jax.sharding import PartitionSpec as P

learn_rate = 0.5
MESH = pl.DeviceIdType.MESH
f32, bf16 = jnp.float32, jnp.bfloat16
buckets = (("gy", 1), ("gx", 1), ("gy", -1))
lanes = 128
least_rows = 16


def matmul(left, right, left_dim, right_dim):
    return lax.dot_general(
        left, right, (((left_dim,), (right_dim,)), ((), ())), preferred_element_type=f32
    )


def chunk_of(count):
    for chunk in (1024, 512, 256, 128):
        if count % chunk == 0:
            return chunk
    return count


def kernel(
    na, nb, divisor, ids, x_in, rel_in, src, dst, base_out, ret_out, rel_out,
    x, xb, fetched, mapped, grads, returned, counts, relb, rel_acc, pieces,
    part_x, part_sum, part_y, gathered,
    fetch_send, fetch_recv, ret_send, ret_recv, rsx_send, rsx_recv, rsy_send, rsy_recv,
    agy_send, agy_recv, agx_send, agx_recv,
):
    a, b = lax.axis_index("gx"), lax.axis_index("gy")
    rounds, groups = ids.shape
    rows, feature = x_in.shape
    kinds = rel_in.shape[0]
    block = rows // groups
    edges = src.shape[1]
    scaling = 1.0 / math.sqrt(rows)
    flat_rows = gathered.shape[0]
    rows_a = flat_rows // na
    owners = min(nb, rows_a // least_rows)
    rows_b = rows_a // owners
    half = kinds * feature

    def owning(position):
        if owners == nb:
            return lambda body: body()
        return pl.when(position < owners)

    def at_x(step):
        return lax.rem(a + step + na, na)

    def at_y(step):
        return lax.rem(b + step + nb, nb)

    barrier = pltpu.get_barrier_semaphore()
    for i in range(1, na):
        pl.semaphore_signal(barrier, inc=1, device_id=(at_x(i), b), device_id_type=MESH)
    for i in range(1, nb):
        pl.semaphore_signal(barrier, inc=1, device_id=(a, at_y(i)), device_id_type=MESH)
    x[...] = x_in[...]
    xb[0] = x_in[...].astype(bf16)
    pl.semaphore_wait(barrier, na + nb - 2)

    def ring(turn, back):
        axis, offset = buckets[turn % len(buckets)]
        step = -offset if back else offset
        return (at_x(step), b) if axis == "gx" else (a, at_y(step))

    def fetch(turn):
        return pltpu.make_async_remote_copy(
            src_ref=xb.at[turn], dst_ref=fetched.at[turn],
            send_sem=fetch_send.at[turn], recv_sem=fetch_recv.at[turn],
            device_id=ring(turn, False), device_id_type=MESH,
        )

    def give_back(turn):
        return pltpu.make_async_remote_copy(
            src_ref=grads.at[turn], dst_ref=returned.at[turn],
            send_sem=ret_send.at[turn], recv_sem=ret_recv.at[turn],
            device_id=ring(turn, True), device_id_type=MESH,
        )

    def count(turn):
        chunk = chunk_of(edges)
        spots = lax.broadcasted_iota(jnp.int32, (rows, chunk), 0).astype(f32).astype(bf16)
        one, zero = jnp.ones((), bf16), jnp.zeros((), bf16)
        total = None
        for start in range(0, edges, chunk):
            s = src[turn : turn + 1, start : start + chunk].astype(f32).astype(bf16)
            t = dst[turn : turn + 1, start : start + chunk].astype(f32).astype(bf16)
            s_hot = jnp.where(spots == s, one, zero)
            t_hot = jnp.where(spots == t, one, zero)
            term = matmul(s_hot, t_hot, 1, 1)
            total = term if total is None else total + term
        counts[...] = total

    fetch(0).start()
    for kind in range(kinds):
        relb[kind] = rel_in[kind].astype(bf16)
    count(0)

    for turn in range(rounds):
        last = turn == rounds - 1
        if turn > 0:
            xb[turn] = x[...].astype(bf16)
            fetch(turn).start()
        for g in range(groups):
            span = slice(g * block, (g + 1) * block)
            mapped[span, :] = matmul(xb[turn, span, :], relb[ids[turn, g]], 1, 0).astype(bf16)
        turned = xb[turn].T
        column = lax.broadcasted_iota(jnp.int32, (1, rows), 1) // block
        kind_of = jnp.zeros((1, rows), jnp.int32)
        for g in range(groups):
            kind_of = jnp.where(column == g, ids[turn, g], kind_of)

        fetch(turn).wait_recv()
        their = fetched[turn]
        scores = matmul(mapped[...], their, 1, 1)
        slopes = ((0.5 * jnp.tanh(0.5 * scores) + 0.5 - counts[...]) * scaling).astype(bf16)

        def pull():
            return matmul(slopes, their, 1, 0).astype(bf16)

        def return_gradient():
            grads[turn] = matmul(slopes, mapped[...], 0, 0).astype(bf16)
            give_back(turn).start()

        def relation_term():
            for kind in range(kinds):
                chosen = turned * (kind_of == kind).astype(f32).astype(bf16)
                term = matmul(chosen, pulled, 1, 0)
                place = slice(kind * feature, (kind + 1) * feature)
                if turn > 0:
                    term = term + rel_acc[place, :]
                rel_acc[place, :] = term / divisor if last else term

        if last:
            pulled = pull()
            relation_term()
            for part in range(feature // lanes):
                pieces[part * half : (part + 1) * half, :] = rel_acc[
                    :, part * lanes : (part + 1) * lanes
                ].astype(bf16)
        else:
            return_gradient()
            pulled = pull()

        if last:
            def scatter_x(i):
                return pltpu.make_async_remote_copy(
                    src_ref=pieces.at[pl.ds(pl.multiple_of(at_x(i) * rows_a, rows_a), rows_a), :],
                    dst_ref=part_x.at[i],
                    send_sem=rsx_send.at[i], recv_sem=rsx_recv.at[i],
                    device_id=(at_x(i), b), device_id_type=MESH,
                )

            for i in range(1, na):
                scatter_x(i).start()
            return_gradient()

        for g in range(groups):
            span = slice(g * block, (g + 1) * block)
            pull_g = pulled[span, :]
            x[span, :] = x[span, :] - learn_rate * matmul(pull_g, relb[ids[turn, g]], 1, 1)
        if not last:
            relation_term()
            count(turn + 1)
            give_back(turn).wait_recv()
            x[...] = x[...] - learn_rate * returned[turn].astype(f32)

    base_out[...] = x[...]

    def scatter_y(i):
        return pltpu.make_async_remote_copy(
            src_ref=part_sum.at[pl.ds(pl.multiple_of(at_y(i) * rows_b, rows_b), rows_b), :],
            dst_ref=part_y.at[i],
            send_sem=rsy_send.at[i], recv_sem=rsy_recv.at[i],
            device_id=(a, at_y(i)), device_id_type=MESH,
        )

    def spot(x_pos, y_pos):
        return gathered.at[
            pl.ds(pl.multiple_of(x_pos * rows_a + y_pos * rows_b, rows_b), rows_b), :
        ]

    def gather_y(i, y_pos):
        return pltpu.make_async_remote_copy(
            src_ref=spot(a, y_pos), dst_ref=spot(a, y_pos),
            send_sem=agy_send.at[i], recv_sem=agy_recv.at[i],
            device_id=(a, at_y(i)), device_id_type=MESH,
        )

    def gather_x(j, i, x_pos, y_pos):
        return pltpu.make_async_remote_copy(
            src_ref=spot(x_pos, y_pos), dst_ref=spot(x_pos, y_pos),
            send_sem=agx_send.at[j, i], recv_sem=agx_recv.at[j, i],
            device_id=(at_x(j), b), device_id_type=MESH,
        )

    own = pieces[pl.ds(pl.multiple_of(a * rows_a, rows_a), rows_a), :].astype(f32)
    for i in range(1, na):
        scatter_x(i).wait_recv()
        own = own + part_x[i].astype(f32)
    part_sum[...] = own.astype(bf16)
    for i in range(1, nb):
        @owning(at_y(i))
        def _():
            scatter_y(i).start()

    @owning(b)
    def _():
        mine = part_sum[pl.ds(pl.multiple_of(b * rows_b, rows_b), rows_b), :].astype(f32)
        for i in range(1, nb):
            scatter_y(i).wait_recv()
            mine = mine + part_y[i].astype(f32)
        gathered[pl.ds(pl.multiple_of(a * rows_a + b * rows_b, rows_b), rows_b), :] = mine.astype(bf16)
        for i in range(1, nb):
            gather_y(i, b).start()
        for j in range(1, na):
            gather_x(j, 0, a, b).start()

    for i in range(1, nb):
        @owning(at_y(-i))
        def _():
            gather_y(i, at_y(-i)).wait_recv()
            for j in range(1, na):
                gather_x(j, i, a, at_y(-i)).start()

    give_back(rounds - 1).wait_recv()
    ret_out[...] = returned[rounds - 1]
    for i in range(nb):
        @owning(at_y(-i))
        def _():
            for j in range(1, na):
                gather_x(j, i, at_x(-j), at_y(-i)).wait_recv()
    rel_out[...] = gathered[...]

    for turn in range(rounds):
        fetch(turn).wait_send()
        give_back(turn).wait_send()
    for i in range(1, na):
        scatter_x(i).wait_send()
    for i in range(1, nb):
        @owning(at_y(i))
        def _():
            scatter_y(i).wait_send()

        @owning(b)
        def _():
            gather_y(i, b).wait_send()
    for i in range(nb):
        @owning(at_y(-i))
        def _():
            for j in range(1, na):
                gather_x(j, i, a, at_y(-i)).wait_send()


def shards(na, nb, entity, relations, rel_ids, edge_src, edge_dst):
    rows, feature = entity.shape
    rounds, groups = rel_ids.shape
    kinds = relations.shape[0]
    flat = kinds * feature * feature // lanes
    rows_a = flat // na
    rows_b = rows_a // min(nb, rows_a // least_rows)
    divisor = math.sqrt(rounds * na * nb)
    dma = pltpu.SemaphoreType.DMA
    in_vmem = pl.BlockSpec(memory_space=pltpu.VMEM)
    base, ret, rel = pl.pallas_call(
        functools.partial(kernel, na, nb, divisor),
        out_shape=(
            jax.ShapeDtypeStruct((rows, feature), f32),
            jax.ShapeDtypeStruct((rows, feature), bf16),
            jax.ShapeDtypeStruct((flat, lanes), bf16),
        ),
        in_specs=[pl.BlockSpec(memory_space=pltpu.SMEM)] + [in_vmem] * 4,
        out_specs=(in_vmem,) * 3,
        scratch_shapes=[
            pltpu.VMEM((rows, feature), f32),
            pltpu.VMEM((rounds, rows, feature), bf16),
            pltpu.VMEM((rounds, rows, feature), bf16),
            pltpu.VMEM((rows, feature), bf16),
            pltpu.VMEM((rounds, rows, feature), bf16),
            pltpu.VMEM((rounds, rows, feature), bf16),
            pltpu.VMEM((rows, rows), f32),
            pltpu.VMEM((kinds, feature, feature), bf16),
            pltpu.VMEM((kinds * feature, feature), f32),
            pltpu.VMEM((flat, lanes), bf16),
            pltpu.VMEM((na, rows_a, lanes), bf16),
            pltpu.VMEM((rows_a, lanes), bf16),
            pltpu.VMEM((nb, rows_b, lanes), bf16),
            pltpu.VMEM((flat, lanes), bf16),
            dma((rounds,)), dma((rounds,)), dma((rounds,)), dma((rounds,)),
            dma((na,)), dma((na,)), dma((nb,)), dma((nb,)),
            dma((nb,)), dma((nb,)), dma((na, nb)), dma((na, nb)),
        ],
        compiler_params=pltpu.CompilerParams(
            collective_id=0, has_side_effects=True, vmem_limit_bytes=40 * 1024 * 1024
        ),
    )(rel_ids, entity, relations, edge_src, edge_dst)
    table = base - learn_rate * ret.astype(f32)
    parts = feature // lanes
    rel = rel.reshape(parts, kinds, feature, lanes).transpose(1, 2, 0, 3)
    return table, rel.reshape(kinds, feature, feature).astype(f32)


def solution(mesh):
    return jax.shard_map(
        functools.partial(shards, mesh.shape["gx"], mesh.shape["gy"]),
        mesh=mesh,
        in_specs=(
            P(("gx", "gy"), None),
            P(),
            P(None, ("gx", "gy")),
            P(None, ("gx", "gy")),
            P(None, ("gx", "gy")),
        ),
        out_specs=(P(("gx", "gy"), None), P()),
        check_vma=False,
    )
```

time: 295 us -> 57.4 us (0.19)
  waiting for transfers between devices: 138 us -> 0 us
  other arithmetic: 107 us -> 1.79 us
  Pallas kernels: 0 us -> 50 us
  matrix products: 19.5 us -> 0 us
  between operations: 14.5 us -> 0.65 us
  starting transfers between devices: 8.27 us -> 0 us
  local copies, waits for them, and re-layouts: 8.32 us -> 4.63 us
    psum x1 -> x0, waiting for transfers between devices: 122 us -> none  [shards(): rel_total = lax.psum(rel_total, ('gx', 'gy'))]
    unnamed x10 -> x0, other arithmetic: 102 us -> none
    pallas_call x0 -> x1, Pallas kernels: none -> 50 us  [shards(): pl.pallas_call(functools.partial(kernel, na, nb, divisor), out_shape=(jax...]
    dot_general x24 -> x0, matrix products: 19.5 us -> none  [the longest x3 7.75 us: shards(): rel_part = jnp.einsum('gk,gde->kde', selector, rel_group, precision=highest)]
    ppermute x6 -> x0, waiting for transfers between devices: 15.8 us -> none  [passed_along(): return lax.ppermute(value, axis, pairs)]
    ppermute x6 -> x0, starting transfers between devices: 8.23 us -> none  [passed_along(): return lax.ppermute(value, axis, pairs)]
  transfers between devices with their start and end apart: 7 -> 0, of which waited for: 4 -> 0; matrix products, arithmetic and copies ran while one was open for 7% -> 0% of each run, Pallas kernels for 0% -> 0%
where the time goes in v1:
time: 57.4 us; the launch traced here: 57.1 us
  Pallas kernels  50 us (87%)
  local copies, waits for them, and re-layouts  4.63 us (8%)
  other arithmetic  1.79 us (3%)
  between operations  0.65 us (1%)
    pallas_call x1, Pallas kernels, shards(): pl.pallas_call(functools.partial(kernel, na, nb, divisor), out_shape=(jax...  50 us
    unnamed x10, local copies, waits for them, and re-layouts  4.63 us

profile of v1, /device:TPU:0, one launch (start us, length us, event | category | flops | bytes accessed | tf_op | source)
XLA Modules:
  0.0 57.1 jit_solution(16710591415520647215)
XLA Ops:
  0.6 0.0 copy-start
  0.6 1.2 %copy-done = f32[4,256,256]{2,1,0:T(8,128)S(1)} copy-done((f32[4,256,256]{2,1,0:T(8,128)S(1)}, f32[4,256,256]{2,1,0:T(8,128)}, u32[]{:S(2)}) %copy-start) | copy-done | bytes 1048600
  1.9 0.0 copy-start.1
  1.9 0.9 %copy-done.1 = f32[256,256]{1,0:T(8,128)S(1)} copy-done((f32[256,256]{1,0:T(8,128)S(1)}, f32[256,256]{1,0:T(8,128)}, u32[]{:S(2)}) %copy-start.1) | copy-done | bytes 262168
  2.8 0.0 copy-start.2
  2.8 0.9 %copy-done.2 = s32[3,6144]{1,0:T(4,128)S(1)} copy-done((s32[3,6144]{1,0:T(4,128)S(1)}, s32[3,6144]{1,0:T(4,128)}, u32[]{:S(2)}) %copy-start.2) | copy-done | bytes 73752
  3.7 0.0 copy-start.3
  3.7 0.9 %copy-done.3 = s32[3,6144]{1,0:T(4,128)S(1)} copy-done((s32[3,6144]{1,0:T(4,128)S(1)}, s32[3,6144]{1,0:T(4,128)}, u32[]{:S(2)}) %copy-start.3) | copy-done | bytes 73752
  4.6 0.0 copy-start.4
  4.6 0.7 %copy-done.4 = s32[3,4]{1,0:T(4,128)S(1)} copy-done((s32[3,4]{1,0:T(4,128)S(1)}, s32[3,4]{1,0:T(4,128)}, u32[]{:S(2)}) %copy-start.4) | copy-done | bytes 72
  5.3 50.0 %shard_map.68 = (f32[256,256]{1,0:T(8,128)S(1)}, bf16[256,256]{1,0:T(8,128)(2,1)S(1)}, bf16[2048,128]{1,0:T(8,128)(2,1)S(1)}) custom-call(s32[3,4]{1,0:T(4,128)S(1)} %copy-done.4, f32[256,256]{1,0:T(8,128)S(1)} %copy-done.1, f32[4,256,256]{2,1,0:T(8,128)S(1)} %copy-done, s32[3,6144]{1,0:T(4,128)S(1)} %copy-done.2, s32[3,6144]{1,0:T(4,128)S(1)} %copy-done.3), custom_call_target="tpu_custom_call" | custom-call | tf_op jit(solution)/shard_map/pallas_call | solution.py:276
  55.3 0.7 %multiply_subtract_fusion = f32[256,256]{1,0:T(8,128)} fusion(f32[256,256]{1,0:T(8,128)S(1)} %get-tuple-element.5, bf16[256,256]{1,0:T(8,128)(2,1)S(1)} %get-tuple-element.6), kind=kLoop, calls=%fused_computation.2 | loop fusion | flops 196608 | bytes 655360 | tf_op jit(solution)/shard_map/sub | solution.py:308
  56.1 1.1 %copy_bitcast_fusion = f32[4,256,256]{2,1,0:T(8,128)} fusion(bf16[2,4,256,128]{3,2,1,0:T(8,128)(2,1)S(1)} %bitcast.8), kind=kLoop, calls=%fused_computation | loop fusion | flops 262144 | bytes 1572864 | tf_op jit(solution)/shard_map/convert_element_type | solution.py:311
Async XLA Ops:
  0.6 1.2 %copy-start = (f32[4,256,256]{2,1,0:T(8,128)S(1)}, f32[4,256,256]{2,1,0:T(8,128)}, u32[]{:S(2)}) copy-start(f32[4,256,256]{2,1,0:T(8,128)} %rel_in.1) | copy-start | bytes 3145732
  1.9 0.9 %copy-start.1 = (f32[256,256]{1,0:T(8,128)S(1)}, f32[256,256]{1,0:T(8,128)}, u32[]{:S(2)}) copy-start(f32[256,256]{1,0:T(8,128)} %x_in.1) | copy-start | bytes 786436
  2.8 0.9 %copy-start.2 = (s32[3,6144]{1,0:T(4,128)S(1)}, s32[3,6144]{1,0:T(4,128)}, u32[]{:S(2)}) copy-start(s32[3,6144]{1,0:T(4,128)} %src.1) | copy-start | bytes 221188
  3.7 0.9 %copy-start.3 = (s32[3,6144]{1,0:T(4,128)S(1)}, s32[3,6144]{1,0:T(4,128)}, u32[]{:S(2)}) copy-start(s32[3,6144]{1,0:T(4,128)} %dst.1) | copy-start | bytes 221188
  4.6 0.7 %copy-start.4 = (s32[3,4]{1,0:T(4,128)S(1)}, s32[3,4]{1,0:T(4,128)}, u32[]{:S(2)}) copy-start(s32[3,4]{1,0:T(4,128)} %ids.1) | copy-start | bytes 148

commit v2 on v1

v2 whole, which is shorter than its diff:
```python
import functools
import math

import jax
import jax.numpy as jnp
from jax import lax
from jax.experimental import pallas as pl
from jax.experimental.pallas import tpu as pltpu
from jax.sharding import PartitionSpec as P

learn_rate = 0.5
MESH = pl.DeviceIdType.MESH
f32, bf16 = jnp.float32, jnp.bfloat16
buckets = (("gy", 1), ("gx", 1), ("gy", -1))
lanes = 128
least_rows = 16


def matmul(left, right, left_dim, right_dim):
    return lax.dot_general(
        left, right, (((left_dim,), (right_dim,)), ((), ())), preferred_element_type=f32
    )


def chunk_of(count):
    for chunk in (1024, 512, 256, 128):
        if count % chunk == 0:
            return chunk
    return count


def kernel(
    na, nb, divisor, ids_in, x_in, rel_in, src_in, dst_in, base_out, ret_out, rel_out,
    ids, rel, src, dst,
    x, xb, fetched, mapped, grads, returned, counts, relb, rel_acc, pieces,
    part_x, part_sum, part_y, gathered,
    load_sem, store_sem,
    fetch_send, fetch_recv, ret_send, ret_recv, rsx_send, rsx_recv, rsy_send, rsy_recv,
    agy_send, agy_recv, agx_send, agx_recv,
):
    a, b = lax.axis_index("gx"), lax.axis_index("gy")
    rounds, groups = ids.shape
    rows, feature = x.shape
    kinds = rel.shape[0]
    block = rows // groups
    edges = src.shape[1]
    scaling = 1.0 / math.sqrt(rows)
    parts = fetch_send.shape[1]
    rows_p = rows // parts
    flat_k = gathered.shape[0] // kinds
    rows_a = flat_k // na
    owners = min(nb, rows_a // least_rows)
    rows_b = rows_a // owners

    loads = [
        pltpu.make_async_copy(source, target, load_sem.at[i])
        for i, (source, target) in enumerate(
            ((x_in, x), (src_in, src), (dst_in, dst), (ids_in, ids), (rel_in, rel))
        )
    ]
    for load in loads:
        load.start()

    def owning(position):
        if owners == nb:
            return lambda body: body()
        return pl.when(position < owners)

    def at_x(step):
        return lax.rem(a + step + na, na)

    def at_y(step):
        return lax.rem(b + step + nb, nb)

    barrier = pltpu.get_barrier_semaphore()
    for i in range(1, na):
        pl.semaphore_signal(barrier, inc=1, device_id=(at_x(i), b), device_id_type=MESH)
    for i in range(1, nb):
        pl.semaphore_signal(barrier, inc=1, device_id=(a, at_y(i)), device_id_type=MESH)

    def ring(turn, back):
        axis, offset = buckets[turn % len(buckets)]
        step = -offset if back else offset
        return (at_x(step), b) if axis == "gx" else (a, at_y(step))

    def part_of(c):
        return slice(c * rows_p, (c + 1) * rows_p)

    def fetch(turn, c):
        here = pl.ds(c * rows_p, rows_p)
        return pltpu.make_async_remote_copy(
            src_ref=xb.at[turn, here, :], dst_ref=fetched.at[turn, here, :],
            send_sem=fetch_send.at[turn, c], recv_sem=fetch_recv.at[turn, c],
            device_id=ring(turn, False), device_id_type=MESH,
        )

    def give_back(turn, c):
        here = pl.ds(c * rows_p, rows_p)
        return pltpu.make_async_remote_copy(
            src_ref=grads.at[turn, here, :], dst_ref=returned.at[turn, here, :],
            send_sem=ret_send.at[turn, c], recv_sem=ret_recv.at[turn, c],
            device_id=ring(turn, True), device_id_type=MESH,
        )

    def count(turn):
        chunk = chunk_of(edges)
        spots = lax.broadcasted_iota(jnp.int32, (rows, chunk), 0).astype(f32).astype(bf16)
        one, zero = jnp.ones((), bf16), jnp.zeros((), bf16)
        total = None
        for start in range(0, edges, chunk):
            s = src[turn : turn + 1, start : start + chunk].astype(f32).astype(bf16)
            t = dst[turn : turn + 1, start : start + chunk].astype(f32).astype(bf16)
            s_hot = jnp.where(spots == s, one, zero)
            t_hot = jnp.where(spots == t, one, zero)
            term = matmul(s_hot, t_hot, 1, 1)
            total = term if total is None else total + term
        counts[...] = total

    def scatter_x(k, i):
        return pltpu.make_async_remote_copy(
            src_ref=pieces.at[pl.ds(pl.multiple_of(k * flat_k + at_x(i) * rows_a, rows_a), rows_a), :],
            dst_ref=part_x.at[k, i],
            send_sem=rsx_send.at[k, i], recv_sem=rsx_recv.at[k, i],
            device_id=(at_x(i), b), device_id_type=MESH,
        )

    def scatter_y(k, i):
        return pltpu.make_async_remote_copy(
            src_ref=part_sum.at[k, pl.ds(pl.multiple_of(at_y(i) * rows_b, rows_b), rows_b), :],
            dst_ref=part_y.at[k, i],
            send_sem=rsy_send.at[k, i], recv_sem=rsy_recv.at[k, i],
            device_id=(a, at_y(i)), device_id_type=MESH,
        )

    def spot(k, y_pos):
        start = k * flat_k + a * rows_a + y_pos * rows_b
        return pl.ds(pl.multiple_of(start, rows_b), rows_b)

    def gather_y(k, i, y_pos):
        return pltpu.make_async_remote_copy(
            src_ref=gathered.at[spot(k, y_pos), :], dst_ref=gathered.at[spot(k, y_pos), :],
            send_sem=agy_send.at[k, i], recv_sem=agy_recv.at[k, i],
            device_id=(a, at_y(i)), device_id_type=MESH,
        )

    def gather_x(k, i, x_pos):
        here = pl.ds(pl.multiple_of(k * flat_k + x_pos * rows_a, rows_a), rows_a)
        return pltpu.make_async_remote_copy(
            src_ref=gathered.at[here, :], dst_ref=gathered.at[here, :],
            send_sem=agx_send.at[k, i], recv_sem=agx_recv.at[k, i],
            device_id=(at_x(i), b), device_id_type=MESH,
        )

    loads[0].wait()
    xb[0] = x[...].astype(bf16)
    pl.semaphore_wait(barrier, na + nb - 2)
    for c in range(parts):
        fetch(0, c).start()
    for load in loads[1:]:
        load.wait()
    for kind in range(kinds):
        relb[kind] = rel[kind].astype(bf16)

    def map_rows(turn):
        for g in range(groups):
            span = slice(g * block, (g + 1) * block)
            mapped[span, :] = matmul(xb[turn, span, :], relb[ids[turn, g]], 1, 0).astype(bf16)

    map_rows(0)
    count(0)

    for turn in range(rounds):
        last = turn == rounds - 1
        if turn > 0:
            map_rows(turn)
        turned = xb[turn].T
        column = lax.broadcasted_iota(jnp.int32, (1, rows), 1) // block
        kind_of = jnp.zeros((1, rows), jnp.int32)
        for g in range(groups):
            kind_of = jnp.where(column == g, ids[turn, g], kind_of)
        here_b = mapped[...]

        slopes = []
        total = None
        for c in range(parts):
            fetch(turn, c).wait_recv()
            their = fetched[turn, part_of(c), :]
            scores = matmul(here_b, their, 1, 1)
            slope = (
                (0.5 * jnp.tanh(0.5 * scores) + 0.5 - counts[:, part_of(c)]) * scaling
            ).astype(bf16)
            slopes.append(slope)
            if not last:
                grads[turn, part_of(c), :] = matmul(slope, here_b, 0, 0).astype(bf16)
                give_back(turn, c).start()
            term = matmul(slope, their, 1, 0)
            total = term if total is None else total + term
        pulled = total.astype(bf16)

        def relation_term():
            for kind in range(kinds):
                chosen = turned * (kind_of == kind).astype(f32).astype(bf16)
                term = matmul(chosen, pulled, 1, 0)
                place = slice(kind * feature, (kind + 1) * feature)
                if turn > 0:
                    term = term + rel_acc[place, :]
                if not last:
                    rel_acc[place, :] = term
                    continue
                term = (term * (1.0 / divisor)).astype(bf16)
                for side in range(feature // lanes):
                    start = kind * flat_k + side * feature
                    pieces[start : start + feature, :] = term[:, side * lanes : (side + 1) * lanes]
                for i in range(1, na):
                    scatter_x(kind, i).start()

        if last:
            relation_term()
            for c in range(parts):
                grads[turn, part_of(c), :] = matmul(slopes[c], here_b, 0, 0).astype(bf16)
                give_back(turn, c).start()
        for g in range(groups):
            span = slice(g * block, (g + 1) * block)
            x[span, :] = x[span, :] - learn_rate * matmul(pulled[span, :], relb[ids[turn, g]], 1, 1)
        if not last:
            relation_term()
            count(turn + 1)
            for c in range(parts):
                give_back(turn, c).wait_recv()
                moved = x[part_of(c), :] - learn_rate * returned[turn, part_of(c), :].astype(f32)
                x[part_of(c), :] = moved
                xb[turn + 1, part_of(c), :] = moved.astype(bf16)
                fetch(turn + 1, c).start()

    store_base = pltpu.make_async_copy(x, base_out, store_sem.at[0])
    store_base.start()

    def reduce_x(k):
        start = k * flat_k + a * rows_a
        own = pieces[pl.ds(pl.multiple_of(start, rows_a), rows_a), :].astype(f32)
        for i in range(1, na):
            scatter_x(k, i).wait_recv()
            own = own + part_x[k, i].astype(f32)
        part_sum[k] = own.astype(bf16)
        for i in range(1, nb):
            @owning(at_y(i))
            def _():
                scatter_y(k, i).start()

    def reduce_y(k):
        @owning(b)
        def _():
            mine = part_sum[k, pl.ds(pl.multiple_of(b * rows_b, rows_b), rows_b), :].astype(f32)
            for i in range(1, nb):
                scatter_y(k, i).wait_recv()
                mine = mine + part_y[k, i].astype(f32)
            gathered[spot(k, b), :] = mine.astype(bf16)
            for i in range(1, nb):
                gather_y(k, i, b).start()

    def spread(k):
        for i in range(1, nb):
            @owning(at_y(-i))
            def _():
                gather_y(k, i, at_y(-i)).wait_recv()
        for i in range(1, na):
            gather_x(k, i, a).start()

    for step in range(kinds + 2):
        if step < kinds:
            reduce_x(step)
        if 0 <= step - 1 < kinds:
            reduce_y(step - 1)
        if 0 <= step - 2:
            spread(step - 2)

    for c in range(parts):
        give_back(rounds - 1, c).wait_recv()
    store_ret = pltpu.make_async_copy(returned.at[rounds - 1], ret_out, store_sem.at[1])
    store_ret.start()
    stores = [store_base, store_ret]
    for k in range(kinds):
        for i in range(1, na):
            gather_x(k, i, at_x(-i)).wait_recv()
        here = pl.ds(k * flat_k, flat_k)
        store = pltpu.make_async_copy(gathered.at[here, :], rel_out.at[here, :], store_sem.at[2 + k])
        store.start()
        stores.append(store)

    for turn in range(rounds):
        for c in range(parts):
            fetch(turn, c).wait_send()
            give_back(turn, c).wait_send()
    for k in range(kinds):
        for i in range(1, na):
            scatter_x(k, i).wait_send()
            gather_x(k, i, a).wait_send()
        for i in range(1, nb):
            @owning(at_y(i))
            def _():
                scatter_y(k, i).wait_send()

            @owning(b)
            def _():
                gather_y(k, i, b).wait_send()
    for store in stores:
        store.wait()


def shards(na, nb, entity, relations, rel_ids, edge_src, edge_dst):
    rows, feature = entity.shape
    rounds, groups = rel_ids.shape
    kinds = relations.shape[0]
    parts = 2
    flat = kinds * feature * feature // lanes
    rows_a = flat // kinds // na
    rows_b = rows_a // min(nb, rows_a // least_rows)
    divisor = math.sqrt(rounds * na * nb)
    dma = pltpu.SemaphoreType.DMA
    in_hbm = pl.BlockSpec(memory_space=pltpu.HBM)
    base, ret, rel = pl.pallas_call(
        functools.partial(kernel, na, nb, divisor),
        out_shape=(
            jax.ShapeDtypeStruct((rows, feature), f32),
            jax.ShapeDtypeStruct((rows, feature), bf16),
            jax.ShapeDtypeStruct((flat, lanes), bf16),
        ),
        in_specs=[in_hbm] * 5,
        out_specs=(in_hbm,) * 3,
        scratch_shapes=[
            pltpu.SMEM(rel_ids.shape, jnp.int32),
            pltpu.VMEM(relations.shape, f32),
            pltpu.VMEM(edge_src.shape, jnp.int32),
            pltpu.VMEM(edge_dst.shape, jnp.int32),
            pltpu.VMEM((rows, feature), f32),
            pltpu.VMEM((rounds, rows, feature), bf16),
            pltpu.VMEM((rounds, rows, feature), bf16),
            pltpu.VMEM((rows, feature), bf16),
            pltpu.VMEM((rounds, rows, feature), bf16),
            pltpu.VMEM((rounds, rows, feature), bf16),
            pltpu.VMEM((rows, rows), f32),
            pltpu.VMEM((kinds, feature, feature), bf16),
            pltpu.VMEM((kinds * feature, feature), f32),
            pltpu.VMEM((flat, lanes), bf16),
            pltpu.VMEM((kinds, na, rows_a, lanes), bf16),
            pltpu.VMEM((kinds, rows_a, lanes), bf16),
            pltpu.VMEM((kinds, nb, rows_b, lanes), bf16),
            pltpu.VMEM((flat, lanes), bf16),
            dma((5,)), dma((2 + kinds,)),
            dma((rounds, parts)), dma((rounds, parts)), dma((rounds, parts)), dma((rounds, parts)),
            dma((kinds, na)), dma((kinds, na)), dma((kinds, nb)), dma((kinds, nb)),
            dma((kinds, nb)), dma((kinds, nb)), dma((kinds, na)), dma((kinds, na)),
        ],
        compiler_params=pltpu.CompilerParams(
            collective_id=0, has_side_effects=True, vmem_limit_bytes=40 * 1024 * 1024
        ),
    )(rel_ids, entity, relations, edge_src, edge_dst)
    table = base - learn_rate * ret.astype(f32)
    sides = feature // lanes
    rel = rel.reshape(kinds, sides, feature, lanes).transpose(0, 2, 1, 3)
    return table, rel.reshape(kinds, feature, feature).astype(f32)


def solution(mesh):
    return jax.shard_map(
        functools.partial(shards, mesh.shape["gx"], mesh.shape["gy"]),
        mesh=mesh,
        in_specs=(
            P(("gx", "gy"), None),
            P(),
            P(None, ("gx", "gy")),
            P(None, ("gx", "gy")),
            P(None, ("gx", "gy")),
        ),
        out_specs=(P(("gx", "gy"), None), P()),
        check_vma=False,
    )
```

time: 57.4 us -> 58.6 us (1.021)
  Pallas kernels: 50 us -> 51.2 us
    pallas_call x1, Pallas kernels: 50 us -> 51.2 us  [shards(): pl.pallas_call(functools.partial(kernel, na, nb, divisor), out_shape=(jax...]
where the time goes in v2:
time: 58.6 us; the launch traced here: 58.3 us
  Pallas kernels  51.2 us (87%)
  local copies, waits for them, and re-layouts  4.63 us (8%)
  other arithmetic  1.79 us (3%)
  between operations  0.65 us (1%)
    pallas_call x1, Pallas kernels, shards(): pl.pallas_call(functools.partial(kernel, na, nb, divisor), out_shape=(jax...  51.2 us
    unnamed x10, local copies, waits for them, and re-layouts  4.63 us

profile of v2, /device:TPU:0, one launch (start us, length us, event | category | flops | bytes accessed | tf_op | source)
XLA Modules:
  0.0 58.3 jit_solution(17337153785483317203)
XLA Ops:
  0.6 0.0 copy-start
  0.6 1.2 %copy-done = f32[4,256,256]{2,1,0:T(8,128)S(1)} copy-done((f32[4,256,256]{2,1,0:T(8,128)S(1)}, f32[4,256,256]{2,1,0:T(8,128)}, u32[]{:S(2)}) %copy-start) | copy-done | bytes 1048600
  1.9 0.0 copy-start.1
  1.9 0.9 %copy-done.1 = f32[256,256]{1,0:T(8,128)S(1)} copy-done((f32[256,256]{1,0:T(8,128)S(1)}, f32[256,256]{1,0:T(8,128)}, u32[]{:S(2)}) %copy-start.1) | copy-done | bytes 262168
  2.8 0.0 copy-start.2
  2.8 0.9 %copy-done.2 = s32[3,6144]{1,0:T(4,128)S(1)} copy-done((s32[3,6144]{1,0:T(4,128)S(1)}, s32[3,6144]{1,0:T(4,128)}, u32[]{:S(2)}) %copy-start.2) | copy-done | bytes 73752
  3.7 0.0 copy-start.3
  3.7 0.9 %copy-done.3 = s32[3,6144]{1,0:T(4,128)S(1)} copy-done((s32[3,6144]{1,0:T(4,128)S(1)}, s32[3,6144]{1,0:T(4,128)}, u32[]{:S(2)}) %copy-start.3) | copy-done | bytes 73752
  4.6 0.0 copy-start.4
  4.6 0.7 %copy-done.4 = s32[3,4]{1,0:T(4,128)S(1)} copy-done((s32[3,4]{1,0:T(4,128)S(1)}, s32[3,4]{1,0:T(4,128)}, u32[]{:S(2)}) %copy-start.4) | copy-done | bytes 72
  5.3 51.2 %shard_map.68 = (f32[256,256]{1,0:T(8,128)S(1)}, bf16[256,256]{1,0:T(8,128)(2,1)S(1)}, bf16[2048,128]{1,0:T(8,128)(2,1)S(1)}) custom-call(s32[3,4]{1,0:T(4,128)S(1)} %copy-done.4, f32[256,256]{1,0:T(8,128)S(1)} %copy-done.1, f32[4,256,256]{2,1,0:T(8,128)S(1)} %copy-done, s32[3,6144]{1,0:T(4,128)S(1)} %copy-done.2, s32[3,6144]{1,0:T(4,128)S(1)} %copy-done.3), custom_call_target="tpu_custom_call" | custom-call | tf_op jit(solution)/shard_map/pallas_call | solution.py:321
  56.5 0.7 %multiply_subtract_fusion = f32[256,256]{1,0:T(8,128)} fusion(f32[256,256]{1,0:T(8,128)S(1)} %get-tuple-element.5, bf16[256,256]{1,0:T(8,128)(2,1)S(1)} %get-tuple-element.6), kind=kLoop, calls=%fused_computation.2 | loop fusion | flops 196608 | bytes 655360 | tf_op jit(solution)/shard_map/sub | solution.py:358
  57.3 1.1 %copy_bitcast_fusion = f32[4,256,256]{2,1,0:T(8,128)} fusion(bf16[4,2,256,128]{3,2,1,0:T(8,128)(2,1)S(1)} %bitcast.8), kind=kLoop, calls=%fused_computation | loop fusion | flops 262144 | bytes 1572864 | tf_op jit(solution)/shard_map/convert_element_type | solution.py:361
Async XLA Ops:
  0.6 1.2 %copy-start = (f32[4,256,256]{2,1,0:T(8,128)S(1)}, f32[4,256,256]{2,1,0:T(8,128)}, u32[]{:S(2)}) copy-start(f32[4,256,256]{2,1,0:T(8,128)} %rel_in.1) | copy-start | bytes 3145732
  1.9 0.9 %copy-start.1 = (f32[256,256]{1,0:T(8,128)S(1)}, f32[256,256]{1,0:T(8,128)}, u32[]{:S(2)}) copy-start(f32[256,256]{1,0:T(8,128)} %x_in.1) | copy-start | bytes 786436
  2.8 0.9 %copy-start.2 = (s32[3,6144]{1,0:T(4,128)S(1)}, s32[3,6144]{1,0:T(4,128)}, u32[]{:S(2)}) copy-start(s32[3,6144]{1,0:T(4,128)} %src_in.1) | copy-start | bytes 221188
  3.7 0.9 %copy-start.3 = (s32[3,6144]{1,0:T(4,128)S(1)}, s32[3,6144]{1,0:T(4,128)}, u32[]{:S(2)}) copy-start(s32[3,6144]{1,0:T(4,128)} %dst_in.1) | copy-start | bytes 221188
  4.6 0.7 %copy-start.4 = (s32[3,4]{1,0:T(4,128)S(1)}, s32[3,4]{1,0:T(4,128)}, u32[]{:S(2)}) copy-start(s32[3,4]{1,0:T(4,128)} %ids_in.1) | copy-start | bytes 148

commit v3 on v2

--- a/solution.py
+++ b/solution.py
@@ -45,9 +45,11 @@
     block = rows // groups
     edges = src.shape[1]
     scaling = 1.0 / math.sqrt(rows)
-    parts = fetch_send.shape[1]
+    parts = fetch_recv.shape[1]
     rows_p = rows // parts
-    flat_k = gathered.shape[0] // kinds
+    chunks = part_x.shape[0]
+    flat = gathered.shape[0]
+    flat_k = flat // chunks
     rows_a = flat_k // na
     owners = min(nb, rows_a // least_rows)
     rows_b = rows_a // owners
@@ -90,7 +92,7 @@
         here = pl.ds(c * rows_p, rows_p)
         return pltpu.make_async_remote_copy(
             src_ref=xb.at[turn, here, :], dst_ref=fetched.at[turn, here, :],
-            send_sem=fetch_send.at[turn, c], recv_sem=fetch_recv.at[turn, c],
+            send_sem=fetch_send.at[0], recv_sem=fetch_recv.at[turn, c],
             device_id=ring(turn, False), device_id_type=MESH,
         )
 
@@ -98,29 +100,50 @@
         here = pl.ds(c * rows_p, rows_p)
         return pltpu.make_async_remote_copy(
             src_ref=grads.at[turn, here, :], dst_ref=returned.at[turn, here, :],
-            send_sem=ret_send.at[turn, c], recv_sem=ret_recv.at[turn, c],
+            send_sem=ret_send.at[0], recv_sem=ret_recv.at[turn, c],
             device_id=ring(turn, True), device_id_type=MESH,
         )
 
-    def count(turn):
+    def await_rows(count, sem):
+        held = gathered.at[pl.ds(0, count), :]
+        pltpu.make_async_copy(held, held, sem).wait()
+
+    def await_owners(weight, sem):
+        if owners == nb:
+            await_rows((nb - 1) * weight, sem)
+            return
+
+        @pl.when(b >= owners)
+        def _():
+            await_rows(owners * weight, sem)
+
+        if owners > 1:
+            @pl.when(b < owners)
+            def _():
+                await_rows((owners - 1) * weight, sem)
+
+    def count(turn, section, sections):
         chunk = chunk_of(edges)
         spots = lax.broadcasted_iota(jnp.int32, (rows, chunk), 0).astype(f32).astype(bf16)
         one, zero = jnp.ones((), bf16), jnp.zeros((), bf16)
         total = None
-        for start in range(0, edges, chunk):
+        starts = range(0, edges, chunk)
+        size = -(-len(starts) // sections)
+        for start in starts[section * size : (section + 1) * size]:
             s = src[turn : turn + 1, start : start + chunk].astype(f32).astype(bf16)
             t = dst[turn : turn + 1, start : start + chunk].astype(f32).astype(bf16)
             s_hot = jnp.where(spots == s, one, zero)
             t_hot = jnp.where(spots == t, one, zero)
             term = matmul(s_hot, t_hot, 1, 1)
             total = term if total is None else total + term
-        counts[...] = total
+        if total is not None:
+            counts[...] = counts[...] + total if section > 0 else total
 
     def scatter_x(k, i):
         return pltpu.make_async_remote_copy(
             src_ref=pieces.at[pl.ds(pl.multiple_of(k * flat_k + at_x(i) * rows_a, rows_a), rows_a), :],
             dst_ref=part_x.at[k, i],
-            send_sem=rsx_send.at[k, i], recv_sem=rsx_recv.at[k, i],
+            send_sem=rsx_send.at[0], recv_sem=rsx_recv.at[k],
             device_id=(at_x(i), b), device_id_type=MESH,
         )
 
@@ -128,7 +151,7 @@
         return pltpu.make_async_remote_copy(
             src_ref=part_sum.at[k, pl.ds(pl.multiple_of(at_y(i) * rows_b, rows_b), rows_b), :],
             dst_ref=part_y.at[k, i],
-            send_sem=rsy_send.at[k, i], recv_sem=rsy_recv.at[k, i],
+            send_sem=rsy_send.at[0], recv_sem=rsy_recv.at[k],
             device_id=(a, at_y(i)), device_id_type=MESH,
         )
 
@@ -139,7 +162,7 @@
     def gather_y(k, i, y_pos):
         return pltpu.make_async_remote_copy(
             src_ref=gathered.at[spot(k, y_pos), :], dst_ref=gathered.at[spot(k, y_pos), :],
-            send_sem=agy_send.at[k, i], recv_sem=agy_recv.at[k, i],
+            send_sem=agy_send.at[0], recv_sem=agy_recv.at[k],
             device_id=(a, at_y(i)), device_id_type=MESH,
         )
 
@@ -147,7 +170,7 @@
         here = pl.ds(pl.multiple_of(k * flat_k + x_pos * rows_a, rows_a), rows_a)
         return pltpu.make_async_remote_copy(
             src_ref=gathered.at[here, :], dst_ref=gathered.at[here, :],
-            send_sem=agx_send.at[k, i], recv_sem=agx_recv.at[k, i],
+            send_sem=agx_send.at[0], recv_sem=agx_recv.at[k],
             device_id=(at_x(i), b), device_id_type=MESH,
         )
 
@@ -167,12 +190,14 @@
             mapped[span, :] = matmul(xb[turn, span, :], relb[ids[turn, g]], 1, 0).astype(bf16)
 
     map_rows(0)
-    count(0)
+    count(0, 0, 1)
 
     for turn in range(rounds):
         last = turn == rounds - 1
         if turn > 0:
             map_rows(turn)
+            relation_term()
+            count(turn, 1, 2)
         turned = xb[turn].T
         column = lax.broadcasted_iota(jnp.int32, (1, rows), 1) // block
         kind_of = jnp.zeros((1, rows), jnp.int32)
@@ -197,7 +222,7 @@
             total = term if total is None else total + term
         pulled = total.astype(bf16)
 
-        def relation_term():
+        def relation_term(turn=turn, last=last, turned=turned, kind_of=kind_of, pulled=pulled):
             for kind in range(kinds):
                 chosen = turned * (kind_of == kind).astype(f32).astype(bf16)
                 term = matmul(chosen, pulled, 1, 0)
@@ -209,10 +234,11 @@
                     continue
                 term = (term * (1.0 / divisor)).astype(bf16)
                 for side in range(feature // lanes):
-                    start = kind * flat_k + side * feature
+                    start = kind * (flat // kinds) + side * feature
                     pieces[start : start + feature, :] = term[:, side * lanes : (side + 1) * lanes]
-                for i in range(1, na):
-                    scatter_x(kind, i).start()
+                if (kind + 1) % (kinds // chunks) == 0:
+                    for i in range(1, na):
+                        scatter_x(kind // (kinds // chunks), i).start()
 
         if last:
             relation_term()
@@ -223,8 +249,7 @@
             span = slice(g * block, (g + 1) * block)
             x[span, :] = x[span, :] - learn_rate * matmul(pulled[span, :], relb[ids[turn, g]], 1, 1)
         if not last:
-            relation_term()
-            count(turn + 1)
+            count(turn + 1, 0, 2)
             for c in range(parts):
                 give_back(turn, c).wait_recv()
                 moved = x[part_of(c), :] - learn_rate * returned[turn, part_of(c), :].astype(f32)
@@ -238,8 +263,8 @@
     def reduce_x(k):
         start = k * flat_k + a * rows_a
         own = pieces[pl.ds(pl.multiple_of(start, rows_a), rows_a), :].astype(f32)
+        await_rows((na - 1) * rows_a, rsx_recv.at[k])
         for i in range(1, na):
-            scatter_x(k, i).wait_recv()
             own = own + part_x[k, i].astype(f32)
         part_sum[k] = own.astype(bf16)
         for i in range(1, nb):
@@ -251,25 +276,22 @@
         @owning(b)
         def _():
             mine = part_sum[k, pl.ds(pl.multiple_of(b * rows_b, rows_b), rows_b), :].astype(f32)
+            await_rows((nb - 1) * rows_b, rsy_recv.at[k])
             for i in range(1, nb):
-                scatter_y(k, i).wait_recv()
                 mine = mine + part_y[k, i].astype(f32)
             gathered[spot(k, b), :] = mine.astype(bf16)
             for i in range(1, nb):
                 gather_y(k, i, b).start()
 
     def spread(k):
-        for i in range(1, nb):
-            @owning(at_y(-i))
-            def _():
-                gather_y(k, i, at_y(-i)).wait_recv()
+        await_owners(rows_b, agy_recv.at[k])
         for i in range(1, na):
             gather_x(k, i, a).start()
 
-    for step in range(kinds + 2):
-        if step < kinds:
+    for step in range(chunks + 2):
+        if step < chunks:
             reduce_x(step)
-        if 0 <= step - 1 < kinds:
+        if 0 <= step - 1 < chunks:
             reduce_y(step - 1)
         if 0 <= step - 2:
             spread(step - 2)
@@ -279,30 +301,23 @@
     store_ret = pltpu.make_async_copy(returned.at[rounds - 1], ret_out, store_sem.at[1])
     store_ret.start()
     stores = [store_base, store_ret]
-    for k in range(kinds):
-        for i in range(1, na):
-            gather_x(k, i, at_x(-i)).wait_recv()
+    for k in range(chunks):
+        await_rows((na - 1) * rows_a, agx_recv.at[k])
         here = pl.ds(k * flat_k, flat_k)
         store = pltpu.make_async_copy(gathered.at[here, :], rel_out.at[here, :], store_sem.at[2 + k])
         store.start()
         stores.append(store)
 
-    for turn in range(rounds):
-        for c in range(parts):
-            fetch(turn, c).wait_send()
-            give_back(turn, c).wait_send()
-    for k in range(kinds):
-        for i in range(1, na):
-            scatter_x(k, i).wait_send()
-            gather_x(k, i, a).wait_send()
-        for i in range(1, nb):
-            @owning(at_y(i))
-            def _():
-                scatter_y(k, i).wait_send()
-
-            @owning(b)
-            def _():
-                gather_y(k, i, b).wait_send()
+    pltpu.make_async_copy(fetched, fetched, fetch_send.at[0]).wait()
+    pltpu.make_async_copy(fetched, fetched, ret_send.at[0]).wait()
+    await_rows(chunks * (na - 1) * rows_a, rsx_send.at[0])
+    await_rows(chunks * (na - 1) * rows_a, agx_send.at[0])
+    await_owners(chunks * rows_b, rsy_send.at[0])
+
+    @owning(b)
+    def _():
+        await_rows(chunks * (nb - 1) * rows_b, agy_send.at[0])
+
     for store in stores:
         store.wait()
 
@@ -312,8 +327,9 @@
     rounds, groups = rel_ids.shape
     kinds = relations.shape[0]
     parts = 2
+    chunks = 2 if kinds % 2 == 0 else 1
     flat = kinds * feature * feature // lanes
-    rows_a = flat // kinds // na
+    rows_a = flat // chunks // na
     rows_b = rows_a // min(nb, rows_a // least_rows)
     divisor = math.sqrt(rounds * na * nb)
     dma = pltpu.SemaphoreType.DMA
@@ -342,17 +358,17 @@
             pltpu.VMEM((kinds, feature, feature), bf16),
             pltpu.VMEM((kinds * feature, feature), f32),
             pltpu.VMEM((flat, lanes), bf16),
-            pltpu.VMEM((kinds, na, rows_a, lanes), bf16),
-            pltpu.VMEM((kinds, rows_a, lanes), bf16),
-            pltpu.VMEM((kinds, nb, rows_b, lanes), bf16),
+            pltpu.VMEM((chunks, na, rows_a, lanes), bf16),
+            pltpu.VMEM((chunks, rows_a, lanes), bf16),
+            pltpu.VMEM((chunks, nb, rows_b, lanes), bf16),
             pltpu.VMEM((flat, lanes), bf16),
-            dma((5,)), dma((2 + kinds,)),
-            dma((rounds, parts)), dma((rounds, parts)), dma((rounds, parts)), dma((rounds, parts)),
-            dma((kinds, na)), dma((kinds, na)), dma((kinds, nb)), dma((kinds, nb)),
-            dma((kinds, nb)), dma((kinds, nb)), dma((kinds, na)), dma((kinds, na)),
+            dma((5,)), dma((2 + chunks,)),
+            dma((1,)), dma((rounds, parts)), dma((1,)), dma((rounds, parts)),
+            dma((1,)), dma((chunks,)), dma((1,)), dma((chunks,)),
+            dma((1,)), dma((chunks,)), dma((1,)), dma((chunks,)),
         ],
         compiler_params=pltpu.CompilerParams(
-            collective_id=0, has_side_effects=True, vmem_limit_bytes=40 * 1024 * 1024
+            collective_id=0, has_side_effects=True, vmem_limit_bytes=64 * 1024 * 1024
         ),
     )(rel_ids, entity, relations, edge_src, edge_dst)
     table = base - learn_rate * ret.astype(f32)

time: 58.6 us -> 48.7 us (0.83)
  Pallas kernels: 51.2 us -> 44.8 us
  local copies, waits for them, and re-layouts: 4.63 us -> 0.01 us
  other arithmetic: 1.79 us -> 2.83 us
    pallas_call x1, Pallas kernels: 51.2 us -> 44.8 us  [shards(): pl.pallas_call(functools.partial(kernel, na, nb, divisor), out_shape=(jax...]
    unnamed x10 -> x2, local copies, waits for them, and re-layouts: 4.63 us -> 0.01 us
    sub x1, other arithmetic: 0.73 us -> 1.77 us  [shards(): table = base - learn_rate * ret.astype(f32)]
where the time goes in v3:
time: 48.7 us; the launch traced here: 48.3 us
  Pallas kernels  44.8 us (92%)
  other arithmetic  2.83 us (6%)
  between operations  0.65 us (1%)
    pallas_call x1, Pallas kernels, shards(): pl.pallas_call(functools.partial(kernel, na, nb, divisor), out_shape=(jax...  44.8 us
    sub x1, other arithmetic, shards(): table = base - learn_rate * ret.astype(f32)  1.77 us
    convert_element_type x1, other arithmetic, shards(): return (table, rel.reshape(kinds, feature, feature).astype(f32))  1.06 us

profile of v3, /device:TPU:0, one launch (start us, length us, event | category | flops | bytes accessed | tf_op | source)
XLA Modules:
  0.0 48.3 jit_solution(7348111050980900871)
XLA Ops:
  0.6 44.8 %shard_map.68 = (f32[256,256]{1,0:T(8,128)}, bf16[256,256]{1,0:T(8,128)(2,1)}, bf16[2048,128]{1,0:T(8,128)(2,1)}) custom-call(s32[3,4]{1,0:T(4,128)} %ids_in.1, f32[256,256]{1,0:T(8,128)} %x_in.1, f32[4,256,256]{2,1,0:T(8,128)} %rel_in.1, s32[3,6144]{1,0:T(4,128)} %src_in.1, s32[3,6144]{1,0:T(4,128)} %dst_in.1), custom_call_target="tpu_custom_call" | custom-call | tf_op jit(solution)/shard_map/pallas_call | solution.py:337
  45.5 0.0 copy-start
  45.5 1.8 %multiply_subtract_fusion = f32[256,256]{1,0:T(8,128)} fusion(f32[256,256]{1,0:T(8,128)} %get-tuple-element.5, bf16[256,256]{1,0:T(8,128)(2,1)} %get-tuple-element.6), kind=kLoop, calls=%fused_computation.2 | loop fusion | flops 196608 | bytes 655360 | tf_op jit(solution)/shard_map/sub | solution.py:374
  47.3 0.0 copy-done
  47.3 1.1 %copy_bitcast_fusion = f32[4,256,256]{2,1,0:T(8,128)} fusion(bf16[4,2,256,128]{3,2,1,0:T(8,128)(2,1)S(1)} %bitcast.8), kind=kLoop, calls=%fused_computation | loop fusion | flops 262144 | bytes 1572864 | tf_op jit(solution)/shard_map/convert_element_type | solution.py:377
Async XLA Ops:
  45.5 1.8 %copy-start = (bf16[2048,128]{1,0:T(8,128)(2,1)S(1)}, bf16[2048,128]{1,0:T(8,128)(2,1)}, u32[]{:S(2)}) copy-start(bf16[2048,128]{1,0:T(8,128)(2,1)} %get-tuple-element.7) | copy-start | bytes 1572868

commit v4 on v3

--- a/solution.py
+++ b/solution.py
@@ -30,13 +30,13 @@
 
 
 def kernel(
-    na, nb, divisor, ids_in, x_in, rel_in, src_in, dst_in, base_out, ret_out, rel_out,
+    na, nb, divisor, ids_in, x_in, rel_in, src_in, dst_in, table_out, rel_out,
     ids, rel, src, dst,
     x, xb, fetched, mapped, grads, returned, counts, relb, rel_acc, pieces,
-    part_x, part_sum, part_y, gathered,
+    part_c, sum_c, part_x, part_sum, part_y, gathered,
     load_sem, store_sem,
-    fetch_send, fetch_recv, ret_send, ret_recv, rsx_send, rsx_recv, rsy_send, rsy_recv,
-    agy_send, agy_recv, agx_send, agx_recv,
+    fetch_send, fetch_recv, ret_send, ret_recv, rsc_send, rsc_recv, rsx_send, rsx_recv,
+    rsy_send, rsy_recv, agy_send, agy_recv, agx_send, agx_recv, agc_send, agc_recv,
 ):
     a, b = lax.axis_index("gx"), lax.axis_index("gy")
     rounds, groups = ids.shape
@@ -68,6 +68,17 @@
             return lambda body: body()
         return pl.when(position < owners)
 
+    side_a = lax.rem(a, 2)
+    pair = lax.div(a, 2)
+    pairs = na // 2
+    sibling = (a + 1 - 2 * side_a, b)
+
+    def same_side(step):
+        return 2 * lax.rem(pair + step + pairs, pairs) + side_a
+
+    def other_side(step):
+        return 2 * lax.rem(pair + step + pairs, pairs) + 1 - side_a
+
     def at_x(step):
         return lax.rem(a + step + na, na)
 
@@ -139,12 +150,21 @@
         if total is not None:
             counts[...] = counts[...] + total if section > 0 else total
 
+    def block_at(k, x_pos):
+        return pl.ds(pl.multiple_of(k * flat_k + x_pos * rows_a, rows_a), rows_a)
+
+    def scatter_c(k, i):
+        return pltpu.make_async_remote_copy(
+            src_ref=pieces.at[block_at(k, other_side(i)), :], dst_ref=part_c.at[k, i],
+            send_sem=rsc_send.at[0], recv_sem=rsc_recv.at[k],
+            device_id=sibling, device_id_type=MESH,
+        )
+
     def scatter_x(k, i):
         return pltpu.make_async_remote_copy(
-            src_ref=pieces.at[pl.ds(pl.multiple_of(k * flat_k + at_x(i) * rows_a, rows_a), rows_a), :],
-            dst_ref=part_x.at[k, i],
+            src_ref=sum_c.at[k, i], dst_ref=part_x.at[k, i],
             send_sem=rsx_send.at[0], recv_sem=rsx_recv.at[k],
-            device_id=(at_x(i), b), device_id_type=MESH,
+            device_id=(same_side(i), b), device_id_type=MESH,
         )
 
     def scatter_y(k, i):
@@ -166,12 +186,20 @@
             device_id=(a, at_y(i)), device_id_type=MESH,
         )
 
-    def gather_x(k, i, x_pos):
-        here = pl.ds(pl.multiple_of(k * flat_k + x_pos * rows_a, rows_a), rows_a)
+    def gather_x(k, i):
+        here = block_at(k, a)
         return pltpu.make_async_remote_copy(
             src_ref=gathered.at[here, :], dst_ref=gathered.at[here, :],
             send_sem=agx_send.at[0], recv_sem=agx_recv.at[k],
-            device_id=(at_x(i), b), device_id_type=MESH,
+            device_id=(same_side(i), b), device_id_type=MESH,
+        )
+
+    def gather_c(k, x_pos):
+        here = block_at(k, x_pos)
+        return pltpu.make_async_remote_copy(
+            src_ref=gathered.at[here, :], dst_ref=gathered.at[here, :],
+            send_sem=agc_send.at[0], recv_sem=agc_recv.at[k],
+            device_id=sibling, device_id_type=MESH,
         )
 
     loads[0].wait()
@@ -237,8 +265,8 @@
                     start = kind * (flat // kinds) + side * feature
                     pieces[start : start + feature, :] = term[:, side * lanes : (side + 1) * lanes]
                 if (kind + 1) % (kinds // chunks) == 0:
-                    for i in range(1, na):
-                        scatter_x(kind // (kinds // chunks), i).start()
+                    for i in range(pairs):
+                        scatter_c(kind // (kinds // chunks), i).start()
 
         if last:
             relation_term()
@@ -257,14 +285,20 @@
                 xb[turn + 1, part_of(c), :] = moved.astype(bf16)
                 fetch(turn + 1, c).start()
 
-    store_base = pltpu.make_async_copy(x, base_out, store_sem.at[0])
-    store_base.start()
+    def pair_sum(k, i):
+        return pieces[block_at(k, same_side(i)), :].astype(f32) + part_c[k, i].astype(f32)
+
+    def reduce_c(k):
+        await_rows(pairs * rows_a, rsc_recv.at[k])
+        for i in range(1, pairs):
+            sum_c[k, i] = pair_sum(k, i).astype(bf16)
+            scatter_x(k, i).start()
 
     def reduce_x(k):
-        start = k * flat_k + a * rows_a
-        own = pieces[pl.ds(pl.multiple_of(start, rows_a), rows_a), :].astype(f32)
-        await_rows((na - 1) * rows_a, rsx_recv.at[k])
-        for i in range(1, na):
+        own = pair_sum(k, 0)
+        if pairs > 1:
+            await_rows((pairs - 1) * rows_a, rsx_recv.at[k])
+        for i in range(1, pairs):
             own = own + part_x[k, i].astype(f32)
         part_sum[k] = own.astype(bf16)
         for i in range(1, nb):
@@ -285,33 +319,43 @@
 
     def spread(k):
         await_owners(rows_b, agy_recv.at[k])
-        for i in range(1, na):
-            gather_x(k, i, a).start()
-
-    for step in range(chunks + 2):
-        if step < chunks:
-            reduce_x(step)
-        if 0 <= step - 1 < chunks:
-            reduce_y(step - 1)
-        if 0 <= step - 2:
-            spread(step - 2)
-
-    for c in range(parts):
-        give_back(rounds - 1, c).wait_recv()
-    store_ret = pltpu.make_async_copy(returned.at[rounds - 1], ret_out, store_sem.at[1])
-    store_ret.start()
-    stores = [store_base, store_ret]
+        for i in range(1, pairs):
+            gather_x(k, i).start()
+        gather_c(k, a).start()
+
+    def forward(k):
+        if pairs > 1:
+            await_rows((pairs - 1) * rows_a, agx_recv.at[k])
+        for i in range(1, pairs):
+            gather_c(k, same_side(-i)).start()
+
+    stages = (reduce_c, reduce_x, reduce_y, spread, forward)
+    for step in range(chunks + len(stages) - 1):
+        if step == chunks + len(stages) - 2:
+            for c in range(parts):
+                give_back(rounds - 1, c).wait_recv()
+            x[...] = x[...] - learn_rate * returned[rounds - 1].astype(f32)
+            store_table = pltpu.make_async_copy(x, table_out, store_sem.at[0])
+            store_table.start()
+        for number, stage in enumerate(stages):
+            if 0 <= step - number < chunks:
+                stage(step - number)
+
+    stores = [store_table]
     for k in range(chunks):
-        await_rows((na - 1) * rows_a, agx_recv.at[k])
+        await_rows(pairs * rows_a, agc_recv.at[k])
         here = pl.ds(k * flat_k, flat_k)
-        store = pltpu.make_async_copy(gathered.at[here, :], rel_out.at[here, :], store_sem.at[2 + k])
+        store = pltpu.make_async_copy(gathered.at[here, :], rel_out.at[here, :], store_sem.at[1 + k])
         store.start()
         stores.append(store)
 
     pltpu.make_async_copy(fetched, fetched, fetch_send.at[0]).wait()
     pltpu.make_async_copy(fetched, fetched, ret_send.at[0]).wait()
-    await_rows(chunks * (na - 1) * rows_a, rsx_send.at[0])
-    await_rows(chunks * (na - 1) * rows_a, agx_send.at[0])
+    await_rows(chunks * pairs * rows_a, rsc_send.at[0])
+    await_rows(chunks * pairs * rows_a, agc_send.at[0])
+    if pairs > 1:
+        await_rows(chunks * (pairs - 1) * rows_a, rsx_send.at[0])
+        await_rows(chunks * (pairs - 1) * rows_a, agx_send.at[0])
     await_owners(chunks * rows_b, rsy_send.at[0])
 
     @owning(b)
@@ -334,15 +378,14 @@
     divisor = math.sqrt(rounds * na * nb)
     dma = pltpu.SemaphoreType.DMA
     in_hbm = pl.BlockSpec(memory_space=pltpu.HBM)
-    base, ret, rel = pl.pallas_call(
+    table, rel = pl.pallas_call(
         functools.partial(kernel, na, nb, divisor),
         out_shape=(
             jax.ShapeDtypeStruct((rows, feature), f32),
-            jax.ShapeDtypeStruct((rows, feature), bf16),
             jax.ShapeDtypeStruct((flat, lanes), bf16),
         ),
         in_specs=[in_hbm] * 5,
-        out_specs=(in_hbm,) * 3,
+        out_specs=(in_hbm,) * 2,
         scratch_shapes=[
             pltpu.SMEM(rel_ids.shape, jnp.int32),
             pltpu.VMEM(relations.shape, f32),
@@ -358,12 +401,15 @@
             pltpu.VMEM((kinds, feature, feature), bf16),
             pltpu.VMEM((kinds * feature, feature), f32),
             pltpu.VMEM((flat, lanes), bf16),
-            pltpu.VMEM((chunks, na, rows_a, lanes), bf16),
+            pltpu.VMEM((chunks, na // 2, rows_a, lanes), bf16),
+            pltpu.VMEM((chunks, na // 2, rows_a, lanes), bf16),
+            pltpu.VMEM((chunks, na // 2, rows_a, lanes), bf16),
             pltpu.VMEM((chunks, rows_a, lanes), bf16),
             pltpu.VMEM((chunks, nb, rows_b, lanes), bf16),
             pltpu.VMEM((flat, lanes), bf16),
-            dma((5,)), dma((2 + chunks,)),
+            dma((5,)), dma((1 + chunks,)),
             dma((1,)), dma((rounds, parts)), dma((1,)), dma((rounds, parts)),
+            dma((1,)), dma((chunks,)), dma((1,)), dma((chunks,)),
             dma((1,)), dma((chunks,)), dma((1,)), dma((chunks,)),
             dma((1,)), dma((chunks,)), dma((1,)), dma((chunks,)),
         ],
@@ -371,7 +417,6 @@
             collective_id=0, has_side_effects=True, vmem_limit_bytes=64 * 1024 * 1024
         ),
     )(rel_ids, entity, relations, edge_src, edge_dst)
-    table = base - learn_rate * ret.astype(f32)
     sides = feature // lanes
     rel = rel.reshape(kinds, sides, feature, lanes).transpose(0, 2, 1, 3)
     return table, rel.reshape(kinds, feature, feature).astype(f32)

time: 48.7 us -> 48.1 us (0.988)
  Pallas kernels: 44.8 us -> 43.9 us
  local copies, waits for them, and re-layouts: 0.01 us -> 0.71 us
  other arithmetic: 2.83 us -> 2.14 us
    sub x1 -> x0, other arithmetic: 1.77 us -> none  [shards(): table = base - learn_rate * ret.astype(f32)]
    convert_element_type x1, other arithmetic: 1.06 us -> 2.14 us  [shards(): return (table, rel.reshape(kinds, feature, feature).astype(f32))]
    pallas_call x1, Pallas kernels: 44.8 us -> 43.9 us  [shards(): pl.pallas_call(functools.partial(kernel, na, nb, divisor), out_shape=(jax...]
    unnamed x2 -> x3, local copies, waits for them, and re-layouts: 0.01 us -> 0.71 us
where the time goes in v4:
time: 48.1 us; the launch traced here: 47.4 us
  Pallas kernels  43.9 us (91%)
  other arithmetic  2.14 us (4%)
  local copies, waits for them, and re-layouts  0.71 us (1%)
  between operations  0.65 us (1%)
    pallas_call x1, Pallas kernels, shards(): pl.pallas_call(functools.partial(kernel, na, nb, divisor), out_shape=(jax...  43.9 us
    convert_element_type x1, other arithmetic, shards(): return (table, rel.reshape(kinds, feature, feature).astype(f32))  2.14 us

profile of v4, /device:TPU:0, one launch (start us, length us, event | category | flops | bytes accessed | tf_op | source)
XLA Modules:
  0.0 47.4 jit_solution(9895199148178938419)
XLA Ops:
  0.6 43.9 %shard_map.68 = (f32[256,256]{1,0:T(8,128)}, bf16[2048,128]{1,0:T(8,128)(2,1)}) custom-call(s32[3,4]{1,0:T(4,128)} %ids_in.1, f32[256,256]{1,0:T(8,128)} %x_in.1, f32[4,256,256]{2,1,0:T(8,128)} %rel_in.1, s32[3,6144]{1,0:T(4,128)} %src_in.1, s32[3,6144]{1,0:T(4,128)} %dst_in.1), custom_call_target="tpu_custom_call" | custom-call | tf_op jit(solution)/shard_map/pallas_call | solution.py:381
  44.5 0.0 copy-start
  44.5 2.1 %copy_bitcast_fusion = f32[4,256,256]{2,1,0:T(8,128)} fusion(bf16[4,2,256,128]{3,2,1,0:T(8,128)(2,1)} %bitcast.8), kind=kLoop, calls=%fused_computation | loop fusion | flops 262144 | bytes 1572864 | tf_op jit(solution)/shard_map/convert_element_type | solution.py:422
  46.6 0.0 copy-done
  46.6 0.7 %copy.11 = f32[256,256]{1,0:T(8,128)} copy(f32[256,256]{1,0:T(8,128)S(1)} %copy-done) | data formatting | bytes 524288
Async XLA Ops:
  44.5 2.2 %copy-start = (f32[256,256]{1,0:T(8,128)S(1)}, f32[256,256]{1,0:T(8,128)}, u32[]{:S(2)}) copy-start(f32[256,256]{1,0:T(8,128)} %get-tuple-element.8) | copy-start | bytes 786436

commit v5 on v4

--- a/solution.py
+++ b/solution.py
@@ -133,22 +133,23 @@
             def _():
                 await_rows((owners - 1) * weight, sem)
 
-    def count(turn, section, sections):
+    def count(turn, first, thirds):
         chunk = chunk_of(edges)
         spots = lax.broadcasted_iota(jnp.int32, (rows, chunk), 0).astype(f32).astype(bf16)
         one, zero = jnp.ones((), bf16), jnp.zeros((), bf16)
         total = None
         starts = range(0, edges, chunk)
-        size = -(-len(starts) // sections)
-        for start in starts[section * size : (section + 1) * size]:
+        cut = len(starts) * thirds // 3
+        for start in starts[:cut] if first else starts[cut:]:
             s = src[turn : turn + 1, start : start + chunk].astype(f32).astype(bf16)
             t = dst[turn : turn + 1, start : start + chunk].astype(f32).astype(bf16)
             s_hot = jnp.where(spots == s, one, zero)
             t_hot = jnp.where(spots == t, one, zero)
             term = matmul(s_hot, t_hot, 1, 1)
             total = term if total is None else total + term
-        if total is not None:
-            counts[...] = counts[...] + total if section > 0 else total
+        if total is None:
+            total = jnp.zeros(counts.shape, f32)
+        counts[...] = total if first else counts[...] + total
 
     def block_at(k, x_pos):
         return pl.ds(pl.multiple_of(k * flat_k + x_pos * rows_a, rows_a), rows_a)
@@ -218,14 +219,15 @@
             mapped[span, :] = matmul(xb[turn, span, :], relb[ids[turn, g]], 1, 0).astype(bf16)
 
     map_rows(0)
-    count(0, 0, 1)
+    count(0, True, 3)
 
     for turn in range(rounds):
         last = turn == rounds - 1
         if turn > 0:
             map_rows(turn)
-            relation_term()
-            count(turn, 1, 2)
+            if not long_way:
+                relation_term()
+            count(turn, False, 2 if long_way else 1)
         turned = xb[turn].T
         column = lax.broadcasted_iota(jnp.int32, (1, rows), 1) // block
         kind_of = jnp.zeros((1, rows), jnp.int32)
@@ -277,7 +279,10 @@
             span = slice(g * block, (g + 1) * block)
             x[span, :] = x[span, :] - learn_rate * matmul(pulled[span, :], relb[ids[turn, g]], 1, 1)
         if not last:
-            count(turn + 1, 0, 2)
+            long_way = buckets[turn % len(buckets)][0] == "gy"
+            if long_way:
+                relation_term()
+            count(turn + 1, True, 2 if long_way else 1)
             for c in range(parts):
                 give_back(turn, c).wait_recv()
                 moved = x[part_of(c), :] - learn_rate * returned[turn, part_of(c), :].astype(f32)

time: 48.1 us -> 50 us (1.040)
  Pallas kernels: 43.9 us -> 45.8 us
    pallas_call x1, Pallas kernels: 43.9 us -> 45.8 us  [shards(): pl.pallas_call(functools.partial(kernel, na, nb, divisor), out_shape=(jax...]
where the time goes in v5:
time: 50 us; the launch traced here: 49.3 us
  Pallas kernels  45.8 us (92%)
  other arithmetic  2.14 us (4%)
  local copies, waits for them, and re-layouts  0.71 us (1%)
  between operations  0.65 us (1%)
    pallas_call x1, Pallas kernels, shards(): pl.pallas_call(functools.partial(kernel, na, nb, divisor), out_shape=(jax...  45.8 us
    convert_element_type x1, other arithmetic, shards(): return (table, rel.reshape(kinds, feature, feature).astype(f32))  2.14 us

profile of v5, /device:TPU:0, one launch (start us, length us, event | category | flops | bytes accessed | tf_op | source)
XLA Modules:
  0.0 49.3 jit_solution(11837958034562716237)
XLA Ops:
  0.6 45.8 %shard_map.68 = (f32[256,256]{1,0:T(8,128)}, bf16[2048,128]{1,0:T(8,128)(2,1)}) custom-call(s32[3,4]{1,0:T(4,128)} %ids_in.1, f32[256,256]{1,0:T(8,128)} %x_in.1, f32[4,256,256]{2,1,0:T(8,128)} %rel_in.1, s32[3,6144]{1,0:T(4,128)} %src_in.1, s32[3,6144]{1,0:T(4,128)} %dst_in.1), custom_call_target="tpu_custom_call" | custom-call | tf_op jit(solution)/shard_map/pallas_call | solution.py:386
  46.4 0.0 copy-start
  46.5 2.1 %copy_bitcast_fusion = f32[4,256,256]{2,1,0:T(8,128)} fusion(bf16[4,2,256,128]{3,2,1,0:T(8,128)(2,1)} %bitcast.8), kind=kLoop, calls=%fused_computation | loop fusion | flops 262144 | bytes 1572864 | tf_op jit(solution)/shard_map/convert_element_type | solution.py:427
  48.6 0.0 copy-done
  48.6 0.7 %copy.11 = f32[256,256]{1,0:T(8,128)} copy(f32[256,256]{1,0:T(8,128)S(1)} %copy-done) | data formatting | bytes 524288
Async XLA Ops:
  46.4 2.2 %copy-start = (f32[256,256]{1,0:T(8,128)S(1)}, f32[256,256]{1,0:T(8,128)}, u32[]{:S(2)}) copy-start(f32[256,256]{1,0:T(8,128)} %get-tuple-element.8) | copy-start | bytes 786436
